TPU v7x, 256 devices: a whole 4x4x8 slice. The times are simulated.
256 devices in a mesh: tensor: 16 (over y, x_lo, core), fsdp: 16 (over x_hi, z).
Axes of the slice: x: 4 (x_hi: 2, x_lo: 2; x = x_hi * 2 + x_lo), y: 4, z: 8, core: 2. Of those that a mesh axis runs over, the one named last changes fastest.
Arguments:
- tokens: bfloat16 [8192, 8192], P('fsdp', 'tensor'), may hold values from -6 to 6
- gate_weight: bfloat16 [8192, 4096], P('fsdp', 'tensor'), may hold values from -0.0625 to 0.0625
- up_weight: bfloat16 [8192, 4096], P('fsdp', 'tensor'), may hold values from -0.0625 to 0.0625
- hidden_grad: bfloat16 [8192, 4096], P('fsdp', 'tensor'), may hold values from -2 to 2
Outputs:
- hidden: bfloat16 [8192, 4096], P('fsdp', 'tensor')
- input_grad: bfloat16 [8192, 8192], P('fsdp', 'tensor')
- gate_grad: float32 [8192, 4096], P('fsdp', 'tensor')
- up_grad: float32 [8192, 4096], P('fsdp', 'tensor')
All inputs are finite; a program needn't handle non-finite values.
Results may differ from a plain program's by a relative error of at most 0.0049.
Values may be sent and summed in bfloat16 or wider, within the bound.
A program may use at most 128 MiB of HBM per device.

v0:
```python
import jax
import jax.numpy as jnp
from jax import lax
from jax.sharding import PartitionSpec as P


def body(tokens, gate_weight, up_weight, hidden_grad):
    width = gate_weight.shape[1]
    paired = jnp.concatenate([gate_weight, up_weight], axis=1)
    full_weights = lax.all_gather(paired, "fsdp", axis=0, tiled=True)
    piece = lax.all_gather(tokens, "tensor", axis=1, tiled=True)
    block = full_weights
    total = jnp.dot(piece, block, preferred_element_type=jnp.float32)
    gate = total[:, :width]
    up = total[:, width:]
    sig = jax.nn.sigmoid(gate)
    active = gate * sig
    hidden = (active * up).astype(jnp.bfloat16)
    upstream = hidden_grad.astype(jnp.float32)
    dgate = (upstream * up * sig * (1.0 + gate * (1.0 - sig))).astype(jnp.bfloat16)
    dup = (upstream * active).astype(jnp.bfloat16)
    grads = jnp.concatenate([dgate, dup], axis=1)
    block = full_weights
    transposed = lax.psum_scatter(
        lax.dot_general(block, grads, (((1,), (1,)), ((), ())), preferred_element_type=jnp.float32),
        "tensor",
        scatter_dimension=0,
        tiled=True,
    )
    input_grad = transposed.T.astype(jnp.bfloat16)
    summed = lax.psum_scatter(
        lax.dot_general(piece, grads, (((0,), (0,)), ((), ())), preferred_element_type=jnp.float32),
        "fsdp",
        scatter_dimension=0,
        tiled=True,
    )
    return (hidden, input_grad, summed[:, :width], summed[:, width:])


def solution(mesh):
    return jax.shard_map(
        body,
        mesh=mesh,
        in_specs=(
            P("fsdp", "tensor"),
            P("fsdp", "tensor"),
            P("fsdp", "tensor"),
            P("fsdp", "tensor"),
        ),
        out_specs=(
            P("fsdp", "tensor"),
            P("fsdp", "tensor"),
            P("fsdp", "tensor"),
            P("fsdp", "tensor"),
        ),
        check_vma=False,
    )
```

profile of v0, /device:TPU:26, one launch (start us, length us, event | category | flops | bytes accessed | tf_op | source)
XLA Modules:
  0.0 701.5 jit_solution(15667632821295600763)
XLA Ops:
  7.2 0.0 all-gather.5.cloned.1.call-start
  7.2 0.7 all-gather.5.cloned.1.call-update
  7.9 0.0 all-gather.3.cloned.1.call-start
  7.9 1.9 pad_maximum_fusion
  9.8 0.0 all-gather.3.cloned.1.call-update
  9.8 0.0 reduce-scatter.5.cloned.1.call-start
  9.9 1.1 copy.8
  11.0 55.5 %all-gather.5.cloned.1.call-done = bf16[512,8192]{1,0:T(8,128)(2,1)} async-done(((bf16[512,512]{1,0:T(8,128)(2,1)}), bf16[512,8192]{1,0:T(8,128)(2,1)}) %all-gather.5.cloned.1.call-update) | async-done | bytes 8388624 | tf_op jit(solution)/shard_map/all_gather | solution.py:11
  66.5 139.8 %all-gather.3.cloned.1.call-done = bf16[8192,512]{1,0:T(8,128)(2,1)} async-done(((bf16[512,512]{1,0:T(8,128)(2,1)}), bf16[8192,512]{1,0:T(8,128)(2,1)}) %all-gather.3.cloned.1.call-update) | async-done | bytes 8388624 | tf_op jit(solution)/shard_map/all_gather | solution.py:10
  206.3 0.0 copy-start
  206.3 9.7 %convolution_bitcast_fusion.1 = f32[512,512]{0,1:T(8,128)S(1)} fusion(bf16[8192,512]{1,0:T(8,128)(2,1)} %all-gather.3.cloned.1.call-done, bf16[512,8192]{1,0:T(8,128)(2,1)} %all-gather.5.cloned.1.call-done), kind=kOutput, calls=%fused_computation.1 | convolution fusion | flops 4294967296 | bytes 17825792 | tf_op jit(solution)/shard_map/dot_general | solution.py:13
  215.9 0.4 fusion.2
  216.3 0.0 copy-done
  216.3 8.1 %convolution_bitcast_fusion = f32[8192,512]{0,1:T(8,128)} fusion(bf16[512,8192]{1,0:T(8,128)(2,1)S(1)} %copy-done, bf16[512,256]{0,1:T(8,128)(2,1)S(1)} %get-tuple-element.9, bf16[512,256]{0,1:T(8,128)(2,1)S(1)} %get-tuple-element.8), kind=kOutput, calls=%fused_computation | convolution fusion | flops 4296015872 | bytes 25690112 | tf_op jit(solution)/shard_map/dot_general | solution.py:32
  224.4 0.0 reduce-scatter.5.cloned.1.call-update
  224.5 0.0 reduce-scatter.3.cloned.1.call-start
  224.5 11.9 %fusion.5 = f32[8192,512]{1,0:T(8,128)} fusion(bf16[8192,512]{1,0:T(8,128)(2,1)} %all-gather.3.cloned.1.call-done, bf16[512,256]{0,1:T(8,128)(2,1)S(1)} %get-tuple-element.9, bf16[512,256]{0,1:T(8,128)(2,1)S(1)} %get-tuple-element.8), kind=kOutput, calls=%fused_computation.14 | convolution fusion | flops 4296015872 | bytes 25690112 | tf_op jit(solution)/shard_map/dot_general | solution.py:25
  236.4 0.0 reduce-scatter.3.cloned.1.call-update
  236.4 0.8 copy.9
  237.2 273.1 %reduce-scatter.5.cloned.1.call-done = f32[512,512]{0,1:T(8,128)} async-done(((f32[8192,512]{0,1:T(8,128)}), f32[512,512]{0,1:T(8,128)}) %reduce-scatter.5.cloned.1.call-update) | async-done | bytes 1048592 | tf_op jit(solution)/shard_map/reduce_scatter | solution.py:31
  510.3 1.3 fusion.8
  511.6 1.0 copy.12
  512.6 1.0 copy.11
  513.6 179.1 %reduce-scatter.3.cloned.1.call-done = f32[512,512]{1,0:T(8,128)} async-done(((f32[8192,512]{1,0:T(8,128)}), f32[512,512]{1,0:T(8,128)}) %reduce-scatter.3.cloned.1.call-update) | async-done | bytes 1048592 | tf_op jit(solution)/shard_map/reduce_scatter | solution.py:24
  692.6 1.3 convert_bitcast_fusion
  693.9 1.0 copy.10
Async XLA Ops:
  7.2 59.4 %all-gather.5.cloned.1.call-start = ((), (), s32[]{:S(2)}) async-start(), calls=%async_computation.3 | async-start | bytes 8912896 | tf_op jit(solution)/shard_map/all_gather | solution.py:11
  7.9 198.4 %all-gather.3.cloned.1.call-start = ((), (), s32[]{:S(2)}) async-start(), calls=%async_computation.2 | async-start | bytes 8912896 | tf_op jit(solution)/shard_map/all_gather | solution.py:10
  9.8 500.5 %reduce-scatter.5.cloned.1.call-start = ((), (), s32[]{:S(2)}) async-start(), calls=%async_computation.5 | async-start | bytes 17825792 | tf_op jit(solution)/shard_map/reduce_scatter | solution.py:31
  206.3 10.0 %copy-start = (bf16[512,8192]{1,0:T(8,128)(2,1)S(1)}, bf16[512,8192]{1,0:T(8,128)(2,1)}, u32[]{:S(2)}) copy-start(bf16[512,8192]{1,0:T(8,128)(2,1)} %all-gather.5.cloned.1.call-done) | copy-start | bytes 25165828
  224.5 468.2 %reduce-scatter.3.cloned.1.call-start = ((), (), s32[]{:S(2)}) async-start(), calls=%async_computation.4 | async-start | bytes 17825792 | tf_op jit(solution)/shard_map/reduce_scatter | solution.py:24
Sparse Core Ops, SparseCore 0:
  9.8 56.6 all-gather.4
  69.7 136.5 all-gather.2
  224.6 285.7 reduce-scatter.4
  512.7 179.8 reduce-scatter.2
where the time goes:
time: 705 us; the launch traced here: 701 us
  waiting for transfers between devices  648 us (92%)
  matrix products  29.6 us (4%)
  between operations  13.8 us (2%)
    reduce_scatter x1, waiting for transfers between devices, body(): lax.psum_scatter(lax.dot_general(piece, grads, (((0,), (0,)), ((), ())),...  273 us
    reduce_scatter x1, waiting for transfers between devices, body(): lax.psum_scatter(lax.dot_general(block, grads, (((1,), (1,)), ((), ())),...  179 us
    all_gather x1, waiting for transfers between devices, body(): full_weights = lax.all_gather(paired, 'fsdp', axis=0, tiled=True)  140 us
    all_gather x1, waiting for transfers between devices, body(): piece = lax.all_gather(tokens, 'tensor', axis=1, tiled=True)  55.5 us
  transfers between devices with their start and end apart: 4, of which 4 were waited for; matrix products, arithmetic and copies ran while one was open for 3% of the time, Pallas kernels for 0%

commit v1 on v0

v1 whole, which is shorter than its diff:
```python
import functools

import jax
import jax.numpy as jnp
from jax import lax
from jax.experimental import pallas as pl
from jax.experimental.pallas import tpu as pltpu
from jax.sharding import PartitionSpec as P

MESH = pl.DeviceIdType.MESH
F32 = jnp.float32
BF16 = jnp.bfloat16
B = 512
H = 256
HALF = (slice(0, H), slice(H, B))
N_SEMS = 80


def kernel(tok, gw, uw, hg, hidden_o, ig_o, gg_o, ug_o,
           t_all, w_all, acc, crecv, dg, igk, igs, igr, y1s, y1r, y2s, y2r, ls, lr, sws, swr, wgb, zs, zr,
           send_sem, recv_sem):
    f = lax.axis_index("fsdp")
    t = lax.axis_index("tensor")
    h, z = f // 8, f % 8
    y, l, c = t // 4, (t // 2) % 2, t % 2
    odd = (y // 2 + h) % 2

    def dev(hh=h, zz=z, yy=y, ll=l, cc=c):
        return {"tensor": (yy % 4) * 4 + ll * 2 + cc, "fsdp": hh * 8 + zz % 8}

    right, left = dev(zz=z + 1), dev(zz=z + 7)
    sib, lnb = dev(cc=1 - c), dev(ll=1 - l)
    yr, yl = dev(yy=y + 1), dev(yy=y + 3)
    swap, hpeer = dev(hh=1 - h, yy=3 - y), dev(hh=1 - h)

    barrier = pltpu.get_barrier_semaphore()
    for d in (right, left, sib, lnb, yr, yl, swap, hpeer):
        pl.semaphore_signal(barrier, inc=1, device_id=d, device_id_type=MESH)
    pl.semaphore_wait(barrier, 8)

    n_used = [0]
    sends = []

    class Copy:
        def __init__(self, src, dst, device, arrives=None):
            k = n_used[0]
            n_used[0] += 1
            assert k < N_SEMS
            make = lambda a, b: pltpu.make_async_remote_copy(
                src_ref=a, dst_ref=b, send_sem=send_sem.at[k], recv_sem=recv_sem.at[k],
                device_id=device, device_id_type=MESH)
            self.out = make(src, dst)
            self.into = make(src, dst if arrives is None else arrives)

        def start(self):
            self.out.start()
            sends.append(self.out)
            return self

        def arrived(self):
            self.into.wait_recv()

    w_all[z, :, :H] = gw[...]
    w_all[z, :, H:] = uw[...]

    def w_copy(way, s, half):
        out, into = ((z + 8 - s) % 8, (z + 7 - s) % 8) if way == 0 else ((z + s) % 8, (z + 1 + s) % 8)
        rows = pl.ds(half * H, H)
        return Copy(w_all.at[out, rows], w_all.at[out, rows], right if way == 0 else left, w_all.at[into, rows])

    w = {}
    for s in range(4):
        for half in range(2):
            for way in range(2):
                if s < 3 or half == way:
                    w[way, s, half] = w_copy(way, s, half)

    def w_start(s, first):
        for k in ((0, 1) if s < 3 else (0,)):
            for way in range(2):
                half = way if k == 0 else 1 - way
                if not first:
                    w[way, s - 1, half].arrived()
                w[way, s, half].start()

    w_start(0, True)

    mine, at_l = t_all.at[t], t_all.at[y * 4 + (1 - l) * 2 + c]
    t_peer = (3 - y) * 4 + l * 2 + c
    swp = Copy(tok, t_all.at[t_peer], swap, mine)

    @pl.when(odd == 1)
    def _():
        swp.out.start()

    @pl.when(odd == 0)
    def _():
        t_all[t] = tok[...]

    @pl.when(odd == 1)
    def _():
        swp.into.wait_recv()

    def slot(yy, ll, cc):
        return (yy % 4) * 4 + ll * 2 + cc

    def to_sib(yy, ll, rows=slice(None)):
        a, b = slot(yy, ll, c), slot(yy, ll, 1 - c)
        r = pl.ds(0, B) if rows == slice(None) else rows
        return Copy(t_all.at[a, r], t_all.at[a, r], sib, t_all.at[b, r]).start()

    def along_y(way, yy, ll, rows):
        src = slot(yy, ll, c)
        into = slot(yy + (3 if way == 0 else 1), ll, c)
        return Copy(t_all.at[src, rows], t_all.at[src, rows], yr if way == 0 else yl, t_all.at[into, rows]).start()

    full, ra, rb = pl.ds(0, B), pl.ds(0, H), pl.ds(H, H)
    from_sib = []
    by_l = Copy(mine, mine, lnb, at_l).start()
    y_own = [along_y(way, y, l, full) for way in range(2)]
    from_sib.append(to_sib(y, l))
    w_start(1, False)
    by_l.arrived()
    y_nbr = [along_y(way, y, 1 - l, full) for way in range(2)]
    from_sib.append(to_sib(y, 1 - l))
    far = []
    for way in range(2):
        y_own[way].arrived()
        yy = y + (3 if way == 0 else 1)
        far.append((way, l, along_y(way, yy, l, ra if way == 0 else rb)))
        from_sib.append(to_sib(yy, l))
    w_start(2, False)
    for way in range(2):
        y_nbr[way].arrived()
        yy = y + (3 if way == 0 else 1)
        far.append((way, 1 - l, along_y(way, yy, 1 - l, ra if way == 0 else rb)))
        from_sib.append(to_sib(yy, 1 - l))
    w_start(3, False)
    for way, ll, copy in far:
        copy.arrived()
        from_sib.append(to_sib(y + 2, ll, ra if way == 0 else rb))
    w[0, 3, 0].arrived()
    w[1, 3, 1].arrived()
    w[0, 2, 1].arrived()
    w[1, 2, 0].arrived()
    for copy in from_sib:
        copy.arrived()

    def place(yy, ll, cc):
        rr = (yy // 2 + h) % 2
        return rr, ((yy + rr) % 2) * 4 + ll * 2 + cc

    def fwd(p, _):
        rr, kb = place(p // 4, (p // 2) % 2, p % 2)
        for n in range(2):
            cols = pl.ds(n * H, H)
            acc[rr, :, cols] += jnp.dot(t_all[p], w_all[kb, :, cols], preferred_element_type=F32)
        return 0

    acc[...] = jnp.zeros_like(acc)
    lax.fori_loop(0, 16, fwd, 0)
    c_part = Copy(acc.at[1], crecv, hpeer).start()
    c_part.arrived()

    def gated(i, _):
        rows = pl.ds(i * 64, 64)
        gate = acc[0, rows, :H] + crecv[rows, :H]
        up = acc[0, rows, H:] + crecv[rows, H:]
        sig = jax.nn.sigmoid(gate)
        active = gate * sig
        upstream = hg[rows].astype(F32)
        hidden_o[rows] = (active * up).astype(BF16)
        dg[0, rows, :H] = (upstream * up * sig * (1.0 + gate * (1.0 - sig))).astype(BF16)
        dg[0, rows, H:] = (upstream * active).astype(BF16)
        return 0

    lax.fori_loop(0, 8, gated, 0)
    d_part = Copy(dg.at[0], dg.at[1], hpeer).start()
    d_part.arrived()

    def ig_block(yy, ll, cc, store):
        rr, kb = place(yy, ll, cc)
        for n in range(2):
            cols = pl.ds(n * H, H)
            store(cols, lax.dot_general(dg[rr], w_all[kb, cols, :], (((1,), (1,)), ((), ())),
                                        preferred_element_type=F32))

    def ig_for_sib(yy):
        yy = yy % 4

        def one(ll, _):
            def store(cols, v):
                igs[yy * 2 + ll, :, cols] = v.astype(BF16)
            ig_block(yy, ll, 1 - c, store)
            return 0
        lax.fori_loop(0, 2, one, 0)
        two = pl.ds(yy * 2, 2)
        return Copy(igs.at[two], igr.at[two], sib).start()

    def ig_own(yy):
        yy = yy % 4

        def one(ll, _):
            def store(cols, v):
                igk[yy * 2 + ll, :, cols] = v
            ig_block(yy, ll, c, store)
            return 0
        lax.fori_loop(0, 2, one, 0)

    def wg_block(j, buf):
        j = j % 8

        for n in range(2):
            ks = pl.ds(n * H, H)
            total = None
            for rr in range(2):
                yy = 2 * ((h + rr) % 2) + (j // 4 + rr) % 2
                v = lax.dot_general(t_all[yy * 4 + j % 4, :, ks], dg[rr], (((0,), (0,)), ((), ())),
                                    preferred_element_type=F32)
                total = v if total is None else total + v
            wgb[buf, ks, :] = total

    def rowwise(start, size, body):
        def one(i, _):
            body(pl.ds(start + i * 64, 64))
            return 0
        lax.fori_loop(0, size // 64, one, 0)

    zc = {}

    def z_send(way, s, half):
        rows = pl.ds(half * H, H)
        zc[way, s, half] = Copy(zs.at[way, s, rows], zr.at[way, s, rows], right if way == 0 else left).start()

    def z_step(way, s, half, buf):
        add = s >= 1 if half == way else s >= 2
        if add:
            zc[way, s - 1, half].arrived()

        def body(rows):
            v = wgb[buf, rows]
            if add:
                v = v + zr[way, s - 1, rows].astype(F32)
            zs[way, s, rows] = v.astype(BF16)
        rowwise(half * H, H, body)
        z_send(way, s, half)

    wg_block(z + 4, 0)
    z_step(0, 0, 0, 0)
    z_step(1, 0, 1, 0)
    sib2 = ig_for_sib(y + 2)
    wg_block(z + 3, 0)
    wg_block(z + 5, 1)
    z_step(0, 1, 1, 0)
    z_step(1, 1, 0, 1)
    ig_own(y + 2)
    sib_near = [ig_for_sib(y + 1), ig_for_sib(y + 3)]
    z_step(0, 1, 0, 0)
    z_step(1, 1, 1, 1)
    sib2.arrived()
    op = ((y + 2) % 4) * 2
    y1 = []
    for way, half in ((0, 0), (1, 1)):
        for ll in range(2):
            def body(rows):
                y1s[ll, rows] = (igk[op + ll, rows] + igr[op + ll, rows].astype(F32)).astype(BF16)
            rowwise(half * H, H, body)
        rows = pl.ds(half * H, H)
        y1.append(Copy(y1s.at[:, rows], y1r.at[:, rows], yr if way == 0 else yl).start())
    ig_own(y + 1)
    ig_own(y + 3)
    y2 = []

    def y_stage(way, half, add):
        near = ((y + (1 if way == 0 else 3)) % 4) * 2
        for ll in range(2):
            def body(rows):
                v = igk[near + ll, rows] + igr[near + ll, rows].astype(F32)
                if add:
                    v = v + y1r[ll, rows].astype(F32)
                y2s[way, ll, rows] = v.astype(BF16)
            rowwise(half * H, H, body)
        rows = pl.ds(half * H, H)
        y2.append((way, Copy(y2s.at[way, :, rows], y2r.at[way, :, rows], yr if way == 0 else yl).start()))

    for way in range(2):
        sib_near[way].arrived()
        y_stage(way, 1 - way, False)
    wg_block(z + 2, 0)
    wg_block(z + 6, 1)
    z_step(0, 2, 1, 0)
    z_step(1, 2, 0, 1)
    z_step(0, 2, 0, 0)
    z_step(1, 2, 1, 1)
    y1[0].arrived()
    y_stage(0, 0, True)
    y1[1].arrived()
    y_stage(1, 1, True)
    sib_own = ig_for_sib(y)
    ig_own(y)
    wg_block(z + 1, 0)
    wg_block(z + 7, 1)
    z_step(0, 3, 1, 0)
    z_step(1, 3, 0, 1)
    z_step(0, 3, 0, 0)
    z_step(1, 3, 1, 1)
    wg_block(z, 0)
    sib_own.arrived()
    for _, copy in y2:
        copy.arrived()

    def y_total(ll, rows):
        v = igk[y * 2 + ll, rows] + igr[y * 2 + ll, rows].astype(F32)
        return v + y2r[0, ll, rows].astype(F32) + y2r[1, ll, rows].astype(F32)

    def body(rows):
        ls[rows] = y_total(1 - l, rows).astype(BF16)
    rowwise(0, B, body)
    l_part = Copy(ls, lr, lnb).start()
    l_part.arrived()

    def body(rows):
        sws[rows] = (y_total(l, rows) + lr[rows].astype(F32)).astype(BF16)
    rowwise(0, B, body)
    back = Copy(sws, swr, swap)

    @pl.when(odd == 1)
    def _():
        back.out.start()

    for half in range(2):
        zc[0, 3, half].arrived()
        zc[1, 3, half].arrived()

    def body(rows):
        v = wgb[0, rows] + zr[0, 3, rows].astype(F32) + zr[1, 3, rows].astype(F32)
        gg_o[rows] = v[:, :H]
        ug_o[rows] = v[:, H:]
    rowwise(0, B, body)

    @pl.when(odd == 0)
    def _():
        ig_o[...] = sws[...]

    @pl.when(odd == 1)
    def _():
        back.into.wait_recv()
        ig_o[...] = swr[...]
        swp.out.wait_send()
        back.out.wait_send()

    for copy in sends:
        copy.wait_send()


def body(tokens, gate_weight, up_weight, hidden_grad):
    vm = pl.BlockSpec(memory_space=pltpu.VMEM)
    return pl.pallas_call(
        kernel,
        out_shape=(
            jax.ShapeDtypeStruct((B, H), BF16),
            jax.ShapeDtypeStruct((B, B), BF16),
            jax.ShapeDtypeStruct((B, H), F32),
            jax.ShapeDtypeStruct((B, H), F32),
        ),
        in_specs=[vm] * 4,
        out_specs=(vm,) * 4,
        scratch_shapes=[
            pltpu.VMEM((16, B, B), BF16),
            pltpu.VMEM((8, B, B), BF16),
            pltpu.VMEM((2, B, B), F32),
            pltpu.VMEM((B, B), F32),
            pltpu.VMEM((2, B, B), BF16),
            pltpu.VMEM((8, B, B), F32),
            pltpu.VMEM((8, B, B), BF16),
            pltpu.VMEM((8, B, B), BF16),
            pltpu.VMEM((2, B, B), BF16),
            pltpu.VMEM((2, B, B), BF16),
            pltpu.VMEM((2, 2, B, B), BF16),
            pltpu.VMEM((2, 2, B, B), BF16),
            pltpu.VMEM((B, B), BF16),
            pltpu.VMEM((B, B), BF16),
            pltpu.VMEM((B, B), BF16),
            pltpu.VMEM((B, B), BF16),
            pltpu.VMEM((2, B, B), F32),
            pltpu.VMEM((2, 4, B, B), BF16),
            pltpu.VMEM((2, 4, B, B), BF16),
            pltpu.SemaphoreType.DMA((N_SEMS,)),
            pltpu.SemaphoreType.DMA((N_SEMS,)),
        ],
        compiler_params=pltpu.CompilerParams(
            collective_id=0, has_side_effects=True, vmem_limit_bytes=60 * 1024 * 1024
        ),
    )(tokens, gate_weight, up_weight, hidden_grad)


def solution(mesh):
    spec = P("fsdp", "tensor")
    return jax.shard_map(body, mesh=mesh, in_specs=(spec,) * 4, out_specs=(spec,) * 4, check_vma=False)
```

time: 705 us -> 185 us (0.26)
  waiting for transfers between devices: 648 us -> 0 us
  Pallas kernels: 0 us -> 177 us
  matrix products: 29.6 us -> 0 us
  between operations: 13.8 us -> 0.65 us
    reduce_scatter x2 -> x0, waiting for transfers between devices: 452 us -> none  [the longest x1 273 us: body(): lax.psum_scatter(lax.dot_general(piece, grads, (((0,), (0,)), ((), ())),...]
    all_gather x2 -> x0, waiting for transfers between devices: 195 us -> none  [the longest x1 140 us: body(): full_weights = lax.all_gather(paired, 'fsdp', axis=0, tiled=True)]
    pallas_call x0 -> x1, Pallas kernels: none -> 177 us  [body(): pl.pallas_call(kernel, out_shape=(jax.ShapeDtypeStruct((B, H), BF16), jax...]
    dot_general x3 -> x0, matrix products: 29.6 us -> none  [the longest x1 11.9 us: body(): lax.dot_general(block, grads, (((1,), (1,)), ((), ())), preferred_element...]
  transfers between devices with their start and end apart: 4 -> 0, of which waited for: 4 -> 0; matrix products, arithmetic and copies ran while one was open for 3% -> 0% of each run, Pallas kernels for 0% -> 0%
where the time goes in v1:
time: 185 us; the launch traced here: 183 us
  Pallas kernels  177 us (96%)
  local copies, waits for them, and re-layouts  4.98 us (3%)
    pallas_call x1, Pallas kernels, body(): pl.pallas_call(kernel, out_shape=(jax.ShapeDtypeStruct((B, H), BF16), jax...  177 us
    unnamed x10, local copies, waits for them, and re-layouts  4.98 us

profile of v1, /device:TPU:26, one launch (start us, length us, event | category | flops | bytes accessed | tf_op | source)
XLA Modules:
  0.0 182.8 jit_solution(3683149488217842582)
XLA Ops:
  0.6 177.1 %shard_map.75 = (bf16[512,256]{1,0:T(8,128)(2,1)}, bf16[512,512]{1,0:T(8,128)(2,1)}, f32[512,256]{1,0:T(8,128)}, f32[512,256]{1,0:T(8,128)}) custom-call(bf16[512,512]{1,0:T(8,128)(2,1)} %tok.1, bf16[512,256]{1,0:T(8,128)(2,1)} %gw.1, bf16[512,256]{1,0:T(8,128)(2,1)} %uw.1, bf16[512,256]{1,0:T(8,128)(2,1)} %hg.1), custom_call_target="tpu_custom_call" | custom-call | tf_op jit(solution)/shard_map/pallas_call | solution.py:358
  177.8 0.0 copy-start.2
  177.8 1.7 copy.12
  179.5 0.0 copy-done.2
  179.5 0.0 copy-start.1
  179.5 0.8 copy.13
  180.3 0.4 copy-done.1
  180.7 0.0 copy-start
  180.7 0.8 copy.14
  181.5 0.4 copy-done
  182.0 0.8 copy.15
Async XLA Ops:
  177.8 1.7 copy-start.2
  179.5 1.2 copy-start.1
  180.7 1.2 copy-start

commit v2 on v1

v2 whole, which is shorter than its diff:
```python
import functools

import jax
import jax.numpy as jnp
from jax import lax
from jax.experimental import pallas as pl
from jax.experimental.pallas import tpu as pltpu
from jax.sharding import PartitionSpec as P

MESH = pl.DeviceIdType.MESH
F32 = jnp.float32
BF16 = jnp.bfloat16
B = 512
H = 256
Q = 128
N_SEMS = 128


def kernel(tok, gw, uw, hg, hidden_o, ig_o, gg_o, ug_o,
           t_all, w_all, acc, cs, cr, dg, igk, igs, igr, ds, dr, es, er, ls, lr, sws, swr, wgb, zs, zr,
           send_sem, recv_sem):
    f = lax.axis_index("fsdp")
    t = lax.axis_index("tensor")
    h, z = f // 8, f % 8
    y, l, c = t // 4, (t // 2) % 2, t % 2
    odd = (y // 2 + h) % 2

    def dev(hh=h, zz=z, yy=y, ll=l, cc=c):
        return {"tensor": (yy % 4) * 4 + ll * 2 + cc, "fsdp": hh * 8 + zz % 8}

    right, left = dev(zz=z + 1), dev(zz=z + 7)
    sib, lnb = dev(cc=1 - c), dev(ll=1 - l)
    yr, yl = dev(yy=y + 1), dev(yy=y + 3)
    swap, hpeer = dev(hh=1 - h, yy=3 - y), dev(hh=1 - h)

    barrier = pltpu.get_barrier_semaphore()
    for d in (right, left, sib, lnb, yr, yl, swap, hpeer):
        pl.semaphore_signal(barrier, inc=1, device_id=d, device_id_type=MESH)
    pl.semaphore_wait(barrier, 8)

    n_used = [0]
    sends = []

    class Copy:
        def __init__(self, src, dst, device, arrives=None):
            self.k = n_used[0]
            n_used[0] += 1
            assert self.k < N_SEMS
            self.src, self.dst, self.device = src, dst, device
            self.into = dst if arrives is None else arrives

        def make(self, src, dst):
            return pltpu.make_async_remote_copy(
                src_ref=src, dst_ref=dst, send_sem=send_sem.at[self.k], recv_sem=recv_sem.at[self.k],
                device_id=self.device, device_id_type=MESH)

        def start(self, listed=True):
            self.make(self.src, self.dst).start()
            if listed and self not in sends:
                sends.append(self)
            return self

        def arrived(self):
            self.make(self.src, self.into).wait_recv()

        def sent(self):
            self.make(self.src, self.dst).wait_send()

    def rowwise(start, size, body):
        def one(i, _):
            body(pl.ds(start + i * 64, 64))
            return 0
        lax.fori_loop(0, size // 64, one, 0)

    for n in range(2):
        part = slice(n * Q, (n + 1) * Q)
        w_all[z, :, n * H:n * H + Q] = gw[:, part]
        w_all[z, :, n * H + Q:(n + 1) * H] = uw[:, part]

    def w_copy(way, s, half):
        out, into = ((z + 8 - s) % 8, (z + 7 - s) % 8) if way == 0 else ((z + s) % 8, (z + 1 + s) % 8)
        rows = pl.ds(half * H, H)
        return Copy(w_all.at[out, rows], w_all.at[out, rows], right if way == 0 else left, w_all.at[into, rows])

    w = {}
    for s in range(4):
        for half in range(2):
            for way in range(2):
                if s < 3 or half == way:
                    w[way, s, half] = w_copy(way, s, half)

    def w_start(s, first):
        for k in ((0, 1) if s < 3 else (0,)):
            for way in range(2):
                half = way if k == 0 else 1 - way
                if not first:
                    w[way, s - 1, half].arrived()
                w[way, s, half].start()

    w_start(0, True)

    mine, at_l = t_all.at[t], t_all.at[y * 4 + (1 - l) * 2 + c]
    t_peer = (3 - y) * 4 + l * 2 + c
    swp = Copy(tok, t_all.at[t_peer], swap, mine)

    @pl.when(odd == 1)
    def _():
        swp.start(False)

    @pl.when(odd == 0)
    def _():
        t_all[t] = tok[...]

    @pl.when(odd == 1)
    def _():
        swp.arrived()

    def slot(yy, ll, cc):
        return (yy % 4) * 4 + ll * 2 + cc

    def to_sib(yy, ll, rows=slice(None)):
        a, b = slot(yy, ll, c), slot(yy, ll, 1 - c)
        r = pl.ds(0, B) if rows == slice(None) else rows
        return Copy(t_all.at[a, r], t_all.at[a, r], sib, t_all.at[b, r]).start()

    def along_y(way, yy, ll, rows):
        src = slot(yy, ll, c)
        into = slot(yy + (3 if way == 0 else 1), ll, c)
        return Copy(t_all.at[src, rows], t_all.at[src, rows], yr if way == 0 else yl, t_all.at[into, rows]).start()

    full, ra, rb = pl.ds(0, B), pl.ds(0, H), pl.ds(H, H)
    from_sib = []
    by_l = Copy(mine, mine, lnb, at_l).start()
    y_own = [along_y(way, y, l, full) for way in range(2)]
    from_sib.append(to_sib(y, l))
    w_start(1, False)
    by_l.arrived()
    y_nbr = [along_y(way, y, 1 - l, full) for way in range(2)]
    from_sib.append(to_sib(y, 1 - l))
    far = []
    for way in range(2):
        y_own[way].arrived()
        yy = y + (3 if way == 0 else 1)
        far.append((way, l, along_y(way, yy, l, ra if way == 0 else rb)))
        from_sib.append(to_sib(yy, l))
    w_start(2, False)
    for way in range(2):
        y_nbr[way].arrived()
        yy = y + (3 if way == 0 else 1)
        far.append((way, 1 - l, along_y(way, yy, 1 - l, ra if way == 0 else rb)))
        from_sib.append(to_sib(yy, 1 - l))
    w_start(3, False)
    w[0, 3, 0].arrived()
    w[1, 3, 1].arrived()
    w[0, 2, 1].arrived()
    w[1, 2, 0].arrived()
    for copy in from_sib:
        copy.arrived()

    def place(yy, ll, cc):
        rr = (yy // 2 + h) % 2
        return rr, ((yy + rr) % 2) * 4 + ll * 2 + cc

    def fwd(yy, parts):
        yy = yy % 4

        def one(i, _):
            rr, kb = place(yy, i // 2, i % 2)
            for n in parts:
                acc[n, rr] += jnp.dot(t_all[yy * 4 + i], w_all[kb, :, n * H:(n + 1) * H], preferred_element_type=F32)
            return 0
        lax.fori_loop(0, 4, one, 0)

    acc[...] = jnp.zeros_like(acc)
    for off in (0, 1, 3):
        fwd(y + off, (0, 1))
    late = []
    for way, ll, copy in far:
        copy.arrived()
        late.append(to_sib(y + 2, ll, ra if way == 0 else rb))
    for copy in late:
        copy.arrived()

    c_part, d_part = [], []
    for n in range(2):
        fwd(y + 2, (n,))

        def body(rows):
            cs[n, rows] = acc[n, 1, rows].astype(cs.dtype)
        rowwise(0, B, body)
        c_part.append(Copy(cs.at[n], cr.at[n], hpeer).start())

    for n in range(2):
        c_part[n].arrived()

        def body(rows):
            v = acc[n, 0, rows] + cr[n, rows].astype(F32)
            gate, up = v[:, :Q], v[:, Q:]
            sig = jax.nn.sigmoid(gate)
            active = gate * sig
            part = slice(n * Q, (n + 1) * Q)
            upstream = hg[rows, part].astype(F32)
            hidden_o[rows, part] = (active * up).astype(BF16)
            dg[n, 0, rows, :Q] = (upstream * up * sig * (1.0 + gate * (1.0 - sig))).astype(BF16)
            dg[n, 0, rows, Q:] = (upstream * active).astype(BF16)
        rowwise(0, B, body)
        d_part.append(Copy(dg.at[n, 0], dg.at[n, 1], hpeer).start())

    sign = 1 - 2 * (y % 2)
    y0, y1 = y + sign, (y - sign + 4) % 4
    d0, d1 = dev(yy=y0), dev(yy=y1)

    def ig_set(r, k):
        target = (odd + r + 1) % 2
        yy = (target * y0 + (1 - target) * ((y + 2) % 4)) if k == 0 else (target * y + (1 - target) * y1)

        def block(ll, cc, store):
            _, kb = place(yy, ll, cc)
            for half in range(2):
                ks = pl.ds(half * H, H)
                total = None
                for n in range(2):
                    v = lax.dot_general(dg[n, r], w_all[kb, ks, n * H:(n + 1) * H], (((1,), (1,)), ((), ())),
                                        preferred_element_type=F32)
                    total = v if total is None else total + v
                store(ll, ks, total)

        def to_other(ll, ks, v):
            igs[r, k, ll, :, ks] = v.astype(BF16)

        def to_own(ll, ks, v):
            igk[r, k, ll, :, ks] = v

        def one(ll, _):
            block(ll, 1 - c, to_other)
            return 0
        lax.fori_loop(0, 2, one, 0)
        copy = Copy(igs.at[r, k], igr.at[r, k], sib).start()

        def one(ll, _):
            block(ll, c, to_own)
            return 0
        lax.fori_loop(0, 2, one, 0)
        return copy

    def both(i, ll, rows, r):
        return igk[r, i, ll, rows] + igr[r, i, ll, rows].astype(F32)

    rows_of = [pl.ds(k * Q, Q) for k in range(4)]
    to_d0 = {(r, k): Copy(ds.at[r, :, rows_of[k]], dr.at[r, :, rows_of[k]], d0) for r in range(2) for k in range(4)}
    to_d1 = [Copy(es.at[:, rows_of[k]], er.at[:, rows_of[k]], d1) for k in range(4)]
    to_l = [Copy(ls.at[rows_of[k]], lr.at[rows_of[k]], lnb) for k in range(4)]
    back = [Copy(sws.at[rows_of[k]], swr.at[rows_of[k]], swap) for k in range(4)]

    def send_d0(r, *parts):
        for k in parts:
            for ll in range(2):
                def body(rows):
                    ds[r, ll, rows] = both(0, ll, rows, r).astype(BF16)
                rowwise(k * Q, Q, body)
            to_d0[r, k].start()

    def send_d1(r, *parts):
        for k in parts:
            to_d0[r, k].arrived()
            for ll in range(2):
                def body(rows):
                    es[ll, rows] = (both(1, ll, rows, r) + dr[r, ll, rows].astype(F32)).astype(BF16)
                rowwise(k * Q, Q, body)
            to_d1[k].start()

    def total(r, ll, rows):
        return both(1, ll, rows, r) + dr[r, ll, rows].astype(F32) + er[ll, rows].astype(F32)

    def send_l(r, *parts):
        for k in parts:
            to_d0[r, k].arrived()
            to_d1[k].arrived()

            def body(rows):
                ls[rows] = total(r, 1 - l, rows).astype(BF16)
            rowwise(k * Q, Q, body)
            to_l[k].start()

    def finish(r, *parts):
        for k in parts:
            to_l[k].arrived()

            def body(rows):
                v = (total(r, l, rows) + lr[rows].astype(F32)).astype(BF16)
                if r == 0:
                    ig_o[rows] = v
                else:
                    sws[rows] = v
            rowwise(k * Q, Q, body)
            if r == 1:
                back[k].start(False)

    def when(is_odd, body, *args):
        @pl.when(odd == is_odd)
        def _():
            body(*args)

    def wg_block(j, buf, n):
        j = j % 8
        for half in range(2):
            ks = pl.ds(half * H, H)
            v = None
            for rr in range(2):
                yy = 2 * ((h + rr) % 2) + (j // 4 + rr) % 2
                u = lax.dot_general(t_all[yy * 4 + j % 4, :, ks], dg[n, rr], (((0,), (0,)), ((), ())),
                                    preferred_element_type=F32)
                v = u if v is None else v + u
            wgb[buf, n, ks, :] = v

    zc = {}

    def z_step(way, s, half, n):
        add = s >= 1 if half == way else s >= 2
        if add:
            zc[way, s - 1, half, n].arrived()

        def body(rows):
            v = wgb[way, n, rows]
            if add:
                v = v + zr[way, s - 1, n, rows].astype(F32)
            zs[way, s, n, rows] = v.astype(BF16)
        rowwise(half * H, H, body)
        rows = pl.ds(half * H, H)
        zc[way, s, half, n] = Copy(zs.at[way, s, n, rows], zr.at[way, s, n, rows], right if way == 0 else left).start()

    def z_begin(n):
        wg_block(z + 4, 0, n)

        def body(rows):
            wgb[1, n, rows] = wgb[0, n, rows]
        rowwise(H, H, body)
        z_step(0, 0, 0, n)
        z_step(1, 0, 1, n)
        z_blocks(1, n)
        z_step(0, 1, 1, n)
        z_step(1, 1, 0, n)

    def z_blocks(s, n):
        wg_block(z + 4 - s, 0, n)
        wg_block(z + 4 + s, 1, n)

    def z_first(n):
        z_step(0, 1, 0, n)
        z_step(1, 1, 1, n)

    def z_next(s, n):
        z_blocks(s, n)
        z_step(0, s, 1, n)
        z_step(1, s, 0, n)
        z_step(0, s, 0, n)
        z_step(1, s, 1, n)

    a0 = ig_set(0, 0)
    d_part[0].arrived()
    z_begin(0)
    a0.arrived()
    send_d0(0, 0, 1)
    when(1, send_d0, 0, 2, 3)
    b0 = ig_set(0, 1)
    d_part[1].arrived()
    a1 = ig_set(1, 0)
    a1.arrived()
    send_d0(1, 0, 1, 2, 3)
    when(0, send_d0, 0, 2, 3)
    z_begin(1)
    z_first(0)
    b0.arrived()
    when(1, send_d1, 0, 0, 1)
    b1 = ig_set(1, 1)
    z_first(1)
    when(1, send_d1, 0, 2, 3)
    z_next(2, 0)
    b1.arrived()
    when(0, send_d1, 1, 0)
    z_next(2, 1)

    def e_1():
        send_l(0, 0)
        send_d1(1, 1)

    def e_2():
        send_l(0, 1)
        send_d1(1, 2)

    def o_2():
        send_l(1, 1)
        finish(1, 0)

    def o_3():
        send_l(1, 2)
        finish(1, 1)

    def e_4():
        finish(0, 0, 1)
        send_l(0, 2, 3)
        finish(0, 2, 3)

    def o_4():
        send_l(1, 3)
        finish(1, 2, 3)

    when(0, e_1)
    when(1, send_l, 1, 0)
    z_next(3, 0)
    when(0, e_2)
    when(1, o_2)
    z_next(3, 1)
    when(0, send_d1, 1, 3)
    when(1, o_3)
    for n in range(2):
        wg_block(z, 0, n)
    when(0, e_4)
    when(1, o_4)
    for n in range(2):
        for half in range(2):
            zc[0, 3, half, n].arrived()
            zc[1, 3, half, n].arrived()

        def body(rows):
            v = wgb[0, n, rows] + zr[0, 3, n, rows].astype(F32) + zr[1, 3, n, rows].astype(F32)
            part = slice(n * Q, (n + 1) * Q)
            gg_o[rows, part] = v[:, :Q]
            ug_o[rows, part] = v[:, Q:]
        rowwise(0, B, body)

    @pl.when(odd == 1)
    def _():
        for k in range(4):
            back[k].arrived()
            ig_o[k * Q:(k + 1) * Q] = swr[k * Q:(k + 1) * Q]
            back[k].sent()
        swp.sent()

    for copy in sends:
        copy.sent()


def body(tokens, gate_weight, up_weight, hidden_grad):
    vm = pl.BlockSpec(memory_space=pltpu.VMEM)
    return pl.pallas_call(
        kernel,
        out_shape=(
            jax.ShapeDtypeStruct((B, H), BF16),
            jax.ShapeDtypeStruct((B, B), BF16),
            jax.ShapeDtypeStruct((B, H), F32),
            jax.ShapeDtypeStruct((B, H), F32),
        ),
        in_specs=[vm] * 4,
        out_specs=(vm,) * 4,
        scratch_shapes=[
            pltpu.VMEM((16, B, B), BF16),
            pltpu.VMEM((8, B, B), BF16),
            pltpu.VMEM((2, 2, B, H), F32),
            pltpu.VMEM((2, B, H), BF16),
            pltpu.VMEM((2, B, H), BF16),
            pltpu.VMEM((2, 2, B, H), BF16),
            pltpu.VMEM((2, 2, 2, B, B), F32),
            pltpu.VMEM((2, 2, 2, B, B), BF16),
            pltpu.VMEM((2, 2, 2, B, B), BF16),
            pltpu.VMEM((2, 2, B, B), BF16),
            pltpu.VMEM((2, 2, B, B), BF16),
            pltpu.VMEM((2, B, B), BF16),
            pltpu.VMEM((2, B, B), BF16),
            pltpu.VMEM((B, B), BF16),
            pltpu.VMEM((B, B), BF16),
            pltpu.VMEM((B, B), BF16),
            pltpu.VMEM((B, B), BF16),
            pltpu.VMEM((2, 2, B, H), F32),
            pltpu.VMEM((2, 4, 2, B, H), BF16),
            pltpu.VMEM((2, 4, 2, B, H), BF16),
            pltpu.SemaphoreType.DMA((N_SEMS,)),
            pltpu.SemaphoreType.DMA((N_SEMS,)),
        ],
        compiler_params=pltpu.CompilerParams(
            collective_id=0, has_side_effects=True, vmem_limit_bytes=60 * 1024 * 1024
        ),
    )(tokens, gate_weight, up_weight, hidden_grad)


def solution(mesh):
    spec = P("fsdp", "tensor")
    return jax.shard_map(body, mesh=mesh, in_specs=(spec,) * 4, out_specs=(spec,) * 4, check_vma=False)
```

time: 185 us -> 155 us (0.84)
  the two profiles are of different devices: /device:TPU:26 before, /device:TPU:5 now
where the time goes in v2:
time: 155 us
  Pallas kernels  150 us (97%)
  local copies, waits for them, and re-layouts  4.98 us (3%)
    pallas_call x1, Pallas kernels, body(): pl.pallas_call(kernel, out_shape=(jax.ShapeDtypeStruct((B, H), BF16), jax...  150 us
    unnamed x10, local copies, waits for them, and re-layouts  4.98 us

profile of v2, /device:TPU:5, one launch (start us, length us, event | category | flops | bytes accessed | tf_op | source)
XLA Modules:
  0.0 155.2 jit_solution(16717757254982461559)
XLA Ops:
  0.6 149.6 %shard_map.75 = (bf16[512,256]{1,0:T(8,128)(2,1)}, bf16[512,512]{1,0:T(8,128)(2,1)}, f32[512,256]{1,0:T(8,128)}, f32[512,256]{1,0:T(8,128)}) custom-call(bf16[512,512]{1,0:T(8,128)(2,1)} %tok.1, bf16[512,256]{1,0:T(8,128)(2,1)} %gw.1, bf16[512,256]{1,0:T(8,128)(2,1)} %uw.1, bf16[512,256]{1,0:T(8,128)(2,1)} %hg.1), custom_call_target="tpu_custom_call" | custom-call | tf_op jit(solution)/shard_map/pallas_call | solution.py:446
  150.2 0.0 copy-start.2
  150.2 1.7 %copy.12 = bf16[512,256]{1,0:T(8,128)(2,1)} copy(bf16[512,256]{1,0:T(8,128)(2,1)} %get-tuple-element.8) | data formatting | bytes 524288
  151.9 0.0 copy-done.2
  151.9 0.0 copy-start.1
  151.9 0.8 copy.13
  152.7 0.4 copy-done.1
  153.2 0.0 copy-start
  153.2 0.8 copy.14
  154.0 0.4 copy-done
  154.4 0.8 copy.15
Async XLA Ops:
  150.2 1.7 %copy-start.2 = (bf16[512,512]{1,0:T(8,128)(2,1)S(1)}, bf16[512,512]{1,0:T(8,128)(2,1)}, u32[]{:S(2)}) copy-start(bf16[512,512]{1,0:T(8,128)(2,1)} %get-tuple-element.9) | copy-start | bytes 1572868
  151.9 1.2 copy-start.1
  153.2 1.2 copy-start

commit v3 on v2

--- a/solution.py
+++ b/solution.py
@@ -17,7 +17,7 @@
 
 
 def kernel(tok, gw, uw, hg, hidden_o, ig_o, gg_o, ug_o,
-           t_all, w_all, acc, cs, cr, dg, igk, igs, igr, ds, dr, es, er, ls, lr, sws, swr, wgb, zs, zr,
+           t_all, w_all, acc, cs, cr, dg, igk, igs, igr, ds, dr, fr, es, er, ls, lr, sws, swr, wgb, zs, zr,
            send_sem, recv_sem):
     f = lax.axis_index("fsdp")
     t = lax.axis_index("tensor")
@@ -89,97 +89,149 @@
                 if s < 3 or half == way:
                     w[way, s, half] = w_copy(way, s, half)
 
-    def w_start(s, first):
-        for k in ((0, 1) if s < 3 else (0,)):
-            for way in range(2):
-                half = way if k == 0 else 1 - way
-                if not first:
-                    w[way, s - 1, half].arrived()
-                w[way, s, half].start()
-
-    w_start(0, True)
-
-    mine, at_l = t_all.at[t], t_all.at[y * 4 + (1 - l) * 2 + c]
-    t_peer = (3 - y) * 4 + l * 2 + c
-    swp = Copy(tok, t_all.at[t_peer], swap, mine)
-
-    @pl.when(odd == 1)
-    def _():
-        swp.start(False)
+    def w_start(s, k):
+        for way in range(2):
+            half = way if k == 0 else 1 - way
+            if s > 0:
+                w[way, s - 1, half].arrived()
+            w[way, s, half].start()
+
+    w_start(0, 0)
+    w_start(0, 1)
+
+    sign = 1 - 2 * (y % 2)
+    y0, y1 = y + sign, (y - sign + 4) % 4
+    d0, d1 = dev(yy=y0), dev(yy=y1)
+    ys = (y, y0, y1, (y + 2) % 4)
+    lls = (l, 1 - l)
+    rows_of = [pl.ds(k * Q, Q) for k in range(4)]
+
+    def slot(i, s, cc=c):
+        return ys[i] * 4 + lls[s] * 2 + cc
+
+    def tcopy(src, rows, device, into):
+        return Copy(t_all.at[src, rows], t_all.at[src, rows], device, t_all.at[into, rows])
+
+    swp = [Copy(tok.at[r], t_all.at[(3 - y) * 4 + l * 2 + c, r], swap, t_all.at[t, r]) for r in rows_of]
+    lx = [tcopy(slot(0, 0), r, lnb, slot(0, 1)) for r in rows_of]
+    yo = {(d, s, k): tcopy(slot(0, s), rows_of[k], (d0, d1)[d], slot(1 + d, s))
+          for d in range(2) for s in range(2) for k in range(4)}
+    fw = {(d, s, k): tcopy(slot(2 - d, s), rows_of[k], (d0, d1)[d], slot(3, s))
+          for d in range(2) for s in range(2) for k in range(4)}
+    sb = {(i, s): tcopy(slot(i, s), pl.ds(0, B), sib, slot(i, s, 1 - c)) for i in range(4) for s in range(2)}
+    by = {0: ((2, 3), (3,)), 1: ((0, 1, 2), (0, 1))}
+    far_in = {0: ((2, 3), (0, 1)), 1: ((0, 1, 2), (3,))}
+
+    def own(k):
+        lx[k].start()
+        yo[0, 0, k].start()
+        yo[1, 0, k].start()
+
+    def near_l(*ks):
+        for k in ks:
+            lx[k].arrived()
+            yo[0, 1, k].start()
+            yo[1, 1, k].start()
+
+    def from_y(kind, d, s, ks=(0, 1, 2, 3)):
+        for k in ks:
+            yo[d, s, k].arrived()
+            if k in by[kind][1 - d]:
+                fw[1 - d, s, k].start(False)
+        if 3 in ks:
+            sb[1 + d, s].start()
+
+    def far_arrived(kind, s):
+        for d in range(2):
+            for k in far_in[kind][d]:
+                fw[d, s, k].arrived()
+        sb[3, s].start()
+
+    def fwd(yy, parts, which=None):
+        yy = yy % 4
+
+        def one(i, _):
+            rr, kb = place(yy, i // 2, i % 2)
+
+            def mm():
+                for n in parts:
+                    acc[n, rr] += jnp.dot(t_all[yy * 4 + i], w_all[kb, :, n * H:(n + 1) * H], preferred_element_type=F32)
+            if which is None:
+                mm()
+            else:
+                early = ((kb - z + 8 + 2) % 8) // 5
+                pl.when(early == which)(mm)
+            return 0
+        lax.fori_loop(0, 4, one, 0)
+
+    def place(yy, ll, cc):
+        rr = (yy // 2 + h) % 2
+        return rr, ((yy + rr) % 2) * 4 + ll * 2 + cc
+
+    acc[...] = jnp.zeros_like(acc)
+
+    def early(other):
+        for i in (0, other):
+            for s in range(2):
+                sb[i, s].arrived()
+            fwd(ys[i], (0, 1), 0)
+        for s in range(2):
+            sb[3 - other, s].arrived()
 
     @pl.when(odd == 0)
     def _():
         t_all[t] = tok[...]
+        for k in range(4):
+            own(k)
+        sb[0, 0].start()
+        w_start(1, 0)
+        from_y(0, 0, 0)
+        near_l(0, 1, 2, 3)
+        sb[0, 1].start()
+        w_start(1, 1)
+        from_y(0, 1, 0, (0, 1))
+        w_start(2, 0)
+        from_y(0, 1, 0, (2, 3))
+        w_start(2, 1)
+        from_y(0, 0, 1)
+        w_start(3, 0)
+        from_y(0, 1, 1)
+        early(1)
+        far_arrived(0, 0)
+        far_arrived(0, 1)
 
     @pl.when(odd == 1)
     def _():
-        swp.arrived()
-
-    def slot(yy, ll, cc):
-        return (yy % 4) * 4 + ll * 2 + cc
-
-    def to_sib(yy, ll, rows=slice(None)):
-        a, b = slot(yy, ll, c), slot(yy, ll, 1 - c)
-        r = pl.ds(0, B) if rows == slice(None) else rows
-        return Copy(t_all.at[a, r], t_all.at[a, r], sib, t_all.at[b, r]).start()
-
-    def along_y(way, yy, ll, rows):
-        src = slot(yy, ll, c)
-        into = slot(yy + (3 if way == 0 else 1), ll, c)
-        return Copy(t_all.at[src, rows], t_all.at[src, rows], yr if way == 0 else yl, t_all.at[into, rows]).start()
-
-    full, ra, rb = pl.ds(0, B), pl.ds(0, H), pl.ds(H, H)
-    from_sib = []
-    by_l = Copy(mine, mine, lnb, at_l).start()
-    y_own = [along_y(way, y, l, full) for way in range(2)]
-    from_sib.append(to_sib(y, l))
-    w_start(1, False)
-    by_l.arrived()
-    y_nbr = [along_y(way, y, 1 - l, full) for way in range(2)]
-    from_sib.append(to_sib(y, 1 - l))
-    far = []
-    for way in range(2):
-        y_own[way].arrived()
-        yy = y + (3 if way == 0 else 1)
-        far.append((way, l, along_y(way, yy, l, ra if way == 0 else rb)))
-        from_sib.append(to_sib(yy, l))
-    w_start(2, False)
-    for way in range(2):
-        y_nbr[way].arrived()
-        yy = y + (3 if way == 0 else 1)
-        far.append((way, 1 - l, along_y(way, yy, 1 - l, ra if way == 0 else rb)))
-        from_sib.append(to_sib(yy, 1 - l))
-    w_start(3, False)
+        for copy in swp:
+            copy.start(False)
+        for k in range(4):
+            swp[k].arrived()
+            own(k)
+            if k % 2:
+                w_start(1, k // 2)
+        sb[0, 0].start()
+        near_l(0, 1, 2, 3)
+        sb[0, 1].start()
+        w_start(2, 0)
+        from_y(1, 1, 0)
+        from_y(1, 0, 0)
+        w_start(2, 1)
+        from_y(1, 1, 1)
+        w_start(3, 0)
+        from_y(1, 0, 1)
+        early(2)
+        far_arrived(1, 0)
+        far_arrived(1, 1)
+
+    w[0, 2, 1].arrived()
+    w[1, 2, 0].arrived()
     w[0, 3, 0].arrived()
     w[1, 3, 1].arrived()
-    w[0, 2, 1].arrived()
-    w[1, 2, 0].arrived()
-    for copy in from_sib:
-        copy.arrived()
-
-    def place(yy, ll, cc):
-        rr = (yy // 2 + h) % 2
-        return rr, ((yy + rr) % 2) * 4 + ll * 2 + cc
-
-    def fwd(yy, parts):
-        yy = yy % 4
-
-        def one(i, _):
-            rr, kb = place(yy, i // 2, i % 2)
-            for n in parts:
-                acc[n, rr] += jnp.dot(t_all[yy * 4 + i], w_all[kb, :, n * H:(n + 1) * H], preferred_element_type=F32)
-            return 0
-        lax.fori_loop(0, 4, one, 0)
-
-    acc[...] = jnp.zeros_like(acc)
-    for off in (0, 1, 3):
-        fwd(y + off, (0, 1))
-    late = []
-    for way, ll, copy in far:
-        copy.arrived()
-        late.append(to_sib(y + 2, ll, ra if way == 0 else rb))
-    for copy in late:
-        copy.arrived()
+    fwd(y, (0, 1), 1)
+    fwd((1 - odd) * y0 + odd * y1, (0, 1), 1)
+    fwd(odd * y0 + (1 - odd) * y1, (0, 1))
+    for s in range(2):
+        sb[3, s].arrived()
 
     c_part, d_part = [], []
     for n in range(2):
@@ -206,10 +258,6 @@
         rowwise(0, B, body)
         d_part.append(Copy(dg.at[n, 0], dg.at[n, 1], hpeer).start())
 
-    sign = 1 - 2 * (y % 2)
-    y0, y1 = y + sign, (y - sign + 4) % 4
-    d0, d1 = dev(yy=y0), dev(yy=y1)
-
     def ig_set(r, k):
         target = (odd + r + 1) % 2
         yy = (target * y0 + (1 - target) * ((y + 2) % 4)) if k == 0 else (target * y + (1 - target) * y1)
@@ -246,26 +294,48 @@
     def both(i, ll, rows, r):
         return igk[r, i, ll, rows] + igr[r, i, ll, rows].astype(F32)
 
-    rows_of = [pl.ds(k * Q, Q) for k in range(4)]
     to_d0 = {(r, k): Copy(ds.at[r, :, rows_of[k]], dr.at[r, :, rows_of[k]], d0) for r in range(2) for k in range(4)}
+    to_d1f = {k: Copy(ds.at[1 - odd, :, rows_of[k]], fr.at[:, rows_of[k]], d1) for k in (2, 3)}
+    by_d1 = {0: (2, 3), 1: (3,)}
     to_d1 = [Copy(es.at[:, rows_of[k]], er.at[:, rows_of[k]], d1) for k in range(4)]
     to_l = [Copy(ls.at[rows_of[k]], lr.at[rows_of[k]], lnb) for k in range(4)]
     back = [Copy(sws.at[rows_of[k]], swr.at[rows_of[k]], swap) for k in range(4)]
 
-    def send_d0(r, *parts):
+    def send_d0(r, *parts, add=False):
+        for k in parts:
+            if add:
+                to_d1f[k].arrived()
+            for ll in range(2):
+                def body(rows):
+                    v = both(0, ll, rows, r)
+                    if add:
+                        v = v + fr[ll, rows].astype(F32)
+                    ds[r, ll, rows] = v.astype(BF16)
+                rowwise(k * Q, Q, body)
+            to_d0[r, k].start(False)
+
+    def send_merged(r, *parts):
+        send_d0(r, *parts, add=True)
+
+    def far_d1(r, *parts):
         for k in parts:
             for ll in range(2):
                 def body(rows):
                     ds[r, ll, rows] = both(0, ll, rows, r).astype(BF16)
                 rowwise(k * Q, Q, body)
-            to_d0[r, k].start()
+            to_d1f[k].start(False)
 
     def send_d1(r, *parts):
         for k in parts:
-            to_d0[r, k].arrived()
+            relay = k not in by_d1[r]
+            if relay:
+                to_d0[r, k].arrived()
             for ll in range(2):
                 def body(rows):
-                    es[ll, rows] = (both(1, ll, rows, r) + dr[r, ll, rows].astype(F32)).astype(BF16)
+                    v = both(1, ll, rows, r)
+                    if relay:
+                        v = v + dr[r, ll, rows].astype(F32)
+                    es[ll, rows] = v.astype(BF16)
                 rowwise(k * Q, Q, body)
             to_d1[k].start()
 
@@ -361,32 +431,26 @@
     z_begin(0)
     a0.arrived()
     send_d0(0, 0, 1)
-    when(1, send_d0, 0, 2, 3)
+    when(1, far_d1, 0, 2, 3)
     b0 = ig_set(0, 1)
     d_part[1].arrived()
     a1 = ig_set(1, 0)
+    b0.arrived()
+    when(1, send_d1, 0, 2, 3)
     a1.arrived()
-    send_d0(1, 0, 1, 2, 3)
-    when(0, send_d0, 0, 2, 3)
+    send_d0(1, 0, 1, 2)
+    when(0, far_d1, 1, 3)
+    b1 = ig_set(1, 1)
+    when(1, send_d1, 0, 0, 1)
     z_begin(1)
+    b1.arrived()
+    when(0, send_d1, 1, 3)
     z_first(0)
-    b0.arrived()
-    when(1, send_d1, 0, 0, 1)
-    b1 = ig_set(1, 1)
+    when(0, send_merged, 0, 2, 3)
+    when(1, send_merged, 1, 3)
     z_first(1)
-    when(1, send_d1, 0, 2, 3)
+    when(0, send_d1, 1, 0)
     z_next(2, 0)
-    b1.arrived()
-    when(0, send_d1, 1, 0)
-    z_next(2, 1)
-
-    def e_1():
-        send_l(0, 0)
-        send_d1(1, 1)
-
-    def e_2():
-        send_l(0, 1)
-        send_d1(1, 2)
 
     def o_2():
         send_l(1, 1)
@@ -397,22 +461,24 @@
         finish(1, 1)
 
     def e_4():
-        finish(0, 0, 1)
+        send_l(0, 1)
+        finish(0, 0)
         send_l(0, 2, 3)
-        finish(0, 2, 3)
+        finish(0, 1, 2, 3)
 
     def o_4():
         send_l(1, 3)
         finish(1, 2, 3)
 
-    when(0, e_1)
+    when(0, send_d1, 1, 1)
     when(1, send_l, 1, 0)
+    z_next(2, 1)
+    when(0, send_d1, 1, 2)
+    when(1, o_2)
     z_next(3, 0)
-    when(0, e_2)
-    when(1, o_2)
+    when(1, o_3)
+    when(0, send_l, 0, 0)
     z_next(3, 1)
-    when(0, send_d1, 1, 3)
-    when(1, o_3)
     for n in range(2):
         wg_block(z, 0, n)
     when(0, e_4)
@@ -435,15 +501,37 @@
             back[k].arrived()
             ig_o[k * Q:(k + 1) * Q] = swr[k * Q:(k + 1) * Q]
             back[k].sent()
-        swp.sent()
 
     for copy in sends:
         copy.sent()
 
+    def sent(kind):
+        for d in range(2):
+            for s in range(2):
+                for k in by[kind][d]:
+                    fw[d, s, k].sent()
+        for r in range(2):
+            for k in range(4):
+                if kind == r or k not in by_d1[r]:
+                    to_d0[r, k].sent()
+        for k in by_d1[1 - kind]:
+            to_d1f[k].sent()
+        if kind == 1:
+            for copy in swp:
+                copy.sent()
+
+    when(0, sent, 0)
+    when(1, sent, 1)
+
+
+def hand_over(*refs):
+    for a, b in zip(refs[:4], refs[4:]):
+        b[...] = a[...]
+
 
 def body(tokens, gate_weight, up_weight, hidden_grad):
     vm = pl.BlockSpec(memory_space=pltpu.VMEM)
-    return pl.pallas_call(
+    results = pl.pallas_call(
         kernel,
         out_shape=(
             jax.ShapeDtypeStruct((B, H), BF16),
@@ -467,6 +555,7 @@
             pltpu.VMEM((2, 2, B, B), BF16),
             pltpu.VMEM((2, B, B), BF16),
             pltpu.VMEM((2, B, B), BF16),
+            pltpu.VMEM((2, B, B), BF16),
             pltpu.VMEM((B, B), BF16),
             pltpu.VMEM((B, B), BF16),
             pltpu.VMEM((B, B), BF16),
@@ -481,6 +570,13 @@
             collective_id=0, has_side_effects=True, vmem_limit_bytes=60 * 1024 * 1024
         ),
     )(tokens, gate_weight, up_weight, hidden_grad)
+    vm4 = [pl.BlockSpec(memory_space=pltpu.VMEM)] * 4
+    return pl.pallas_call(
+        hand_over,
+        out_shape=[jax.ShapeDtypeStruct(r.shape, r.dtype) for r in results],
+        in_specs=vm4,
+        out_specs=vm4,
+    )(*results)
 
 
 def solution(mesh):

time: 155 us -> 145 us (0.935)
  the two profiles are of different devices: /device:TPU:5 before, /device:TPU:26 now
where the time goes in v3:
time: 145 us; the launch traced here: 144 us
  Pallas kernels  143 us (99%)
    pallas_call x1, Pallas kernels, body(): pl.pallas_call(kernel, out_shape=(jax.ShapeDtypeStruct((B, H), BF16), jax...  141 us

profile of v3, /device:TPU:26, one launch (start us, length us, event | category | flops | bytes accessed | tf_op | source)
XLA Modules:
  0.0 144.0 jit_solution(12840033586811883459)
XLA Ops:
  0.6 140.6 %shard_map.75 = (bf16[512,256]{1,0:T(8,128)(2,1)}, bf16[512,512]{1,0:T(8,128)(2,1)}, f32[512,256]{1,0:T(8,128)}, f32[512,256]{1,0:T(8,128)}) custom-call(bf16[512,512]{1,0:T(8,128)(2,1)} %tok.1, bf16[512,256]{1,0:T(8,128)(2,1)} %gw.1, bf16[512,256]{1,0:T(8,128)(2,1)} %uw.1, bf16[512,256]{1,0:T(8,128)(2,1)} %hg.1), custom_call_target="tpu_custom_call" | custom-call | tf_op jit(solution)/shard_map/pallas_call | solution.py:534
  141.3 2.7 %shard_map.76 = (bf16[512,256]{1,0:T(8,128)(2,1)}, bf16[512,512]{1,0:T(8,128)(2,1)}, f32[512,256]{1,0:T(8,128)}, f32[512,256]{1,0:T(8,128)}) custom-call(bf16[512,256]{1,0:T(8,128)(2,1)} %get-tuple-element.8.refs_0_, bf16[512,512]{1,0:T(8,128)(2,1)} %get-tuple-element.9.refs_1_, f32[512,256]{1,0:T(8,128)} %get-tuple-element.10.refs_2_, ...), custom_call_target="tpu_custom_call" | custom-call | tf_op jit(solution)/shard_map/pallas_call | solution.py:574

commit v4 on v3

--- a/solution.py
+++ b/solution.py
@@ -168,9 +168,8 @@
         rr = (yy // 2 + h) % 2
         return rr, ((yy + rr) % 2) * 4 + ll * 2 + cc
 
-    acc[...] = jnp.zeros_like(acc)
-
     def early(other):
+        acc[...] = jnp.zeros_like(acc)
         for i in (0, other):
             for s in range(2):
                 sb[i, s].arrived()
@@ -227,21 +226,46 @@
     w[1, 2, 0].arrived()
     w[0, 3, 0].arrived()
     w[1, 3, 1].arrived()
-    fwd(y, (0, 1), 1)
-    fwd((1 - odd) * y0 + odd * y1, (0, 1), 1)
-    fwd(odd * y0 + (1 - odd) * y1, (0, 1))
-    for s in range(2):
-        sb[3, s].arrived()
 
     c_part, d_part = [], []
+    def when(is_odd, body, *args):
+        @pl.when(odd == is_odd)
+        def _():
+            body(*args)
+
+    def far_here():
+        for s in range(2):
+            sb[3, s].arrived()
+
+    def other_even(n):
+        fwd(y1, (n,))
+        fwd(ys[3], (n,))
+
+    def other_odd(n):
+        fwd(y, (n,), 1)
+        fwd(y0, (n,))
+
+    def own_even():
+        fwd(y, (0, 1), 1)
+        fwd(y0, (0, 1), 1)
+
+    def own_odd():
+        far_here()
+        fwd(y1, (0, 1), 1)
+        fwd(ys[3], (0, 1))
+
+    when(0, far_here)
     for n in range(2):
-        fwd(y + 2, (n,))
+        when(0, other_even, n)
+        when(1, other_odd, n)
 
         def body(rows):
             cs[n, rows] = acc[n, 1, rows].astype(cs.dtype)
         rowwise(0, B, body)
         c_part.append(Copy(cs.at[n], cr.at[n], hpeer).start())
 
+    when(0, own_even)
+    when(1, own_odd)
     for n in range(2):
         c_part[n].arrived()
 
@@ -365,11 +389,6 @@
             rowwise(k * Q, Q, body)
             if r == 1:
                 back[k].start(False)
-
-    def when(is_odd, body, *args):
-        @pl.when(odd == is_odd)
-        def _():
-            body(*args)
 
     def wg_block(j, buf, n):
         j = j % 8

time: 145 us -> 143 us (0.986)
    pallas_call x1, Pallas kernels: 141 us -> 139 us  [body(): pl.pallas_call(kernel, out_shape=(jax.ShapeDtypeStruct((B, H), BF16), jax...]
where the time goes in v4:
time: 143 us; the launch traced here: 142 us
  Pallas kernels  142 us (99%)
    pallas_call x1, Pallas kernels, body(): pl.pallas_call(kernel, out_shape=(jax.ShapeDtypeStruct((B, H), BF16), jax...  139 us

profile of v4, /device:TPU:26, one launch (start us, length us, event | category | flops | bytes accessed | tf_op | source)
XLA Modules:
  0.0 142.4 jit_solution(4368870381319106658)
XLA Ops:
  0.6 139.1 %shard_map.75 = (bf16[512,256]{1,0:T(8,128)(2,1)}, bf16[512,512]{1,0:T(8,128)(2,1)}, f32[512,256]{1,0:T(8,128)}, f32[512,256]{1,0:T(8,128)}) custom-call(bf16[512,512]{1,0:T(8,128)(2,1)} %tok.1, bf16[512,256]{1,0:T(8,128)(2,1)} %gw.1, bf16[512,256]{1,0:T(8,128)(2,1)} %uw.1, bf16[512,256]{1,0:T(8,128)(2,1)} %hg.1), custom_call_target="tpu_custom_call" | custom-call | tf_op jit(solution)/shard_map/pallas_call | solution.py:553
  139.7 2.7 %shard_map.76 = (bf16[512,256]{1,0:T(8,128)(2,1)}, bf16[512,512]{1,0:T(8,128)(2,1)}, f32[512,256]{1,0:T(8,128)}, f32[512,256]{1,0:T(8,128)}) custom-call(bf16[512,256]{1,0:T(8,128)(2,1)} %get-tuple-element.8.refs_0_, bf16[512,512]{1,0:T(8,128)(2,1)} %get-tuple-element.9.refs_1_, f32[512,256]{1,0:T(8,128)} %get-tuple-element.10.refs_2_, ...), custom_call_target="tpu_custom_call" | custom-call | tf_op jit(solution)/shard_map/pallas_call | solution.py:593

commit v5 on v4

--- a/solution.py
+++ b/solution.py
@@ -454,6 +454,7 @@
     b0 = ig_set(0, 1)
     d_part[1].arrived()
     a1 = ig_set(1, 0)
+    z_begin(1)
     b0.arrived()
     when(1, send_d1, 0, 2, 3)
     a1.arrived()
@@ -461,7 +462,6 @@
     when(0, far_d1, 1, 3)
     b1 = ig_set(1, 1)
     when(1, send_d1, 0, 0, 1)
-    z_begin(1)
     b1.arrived()
     when(0, send_d1, 1, 3)
     z_first(0)

time: 143 us -> 144 us (level)
  no operation moved by 1% of the time
where the time goes in v5:
time: 144 us; the launch traced here: 143 us
  Pallas kernels  143 us (99%)
    pallas_call x1, Pallas kernels, body(): pl.pallas_call(kernel, out_shape=(jax.ShapeDtypeStruct((B, H), BF16), jax...  140 us

profile of v5, /device:TPU:26, one launch (start us, length us, event | category | flops | bytes accessed | tf_op | source)
XLA Modules:
  0.0 143.3 jit_solution(13087850623964739196)
XLA Ops:
  0.6 139.9 %shard_map.75 = (bf16[512,256]{1,0:T(8,128)(2,1)}, bf16[512,512]{1,0:T(8,128)(2,1)}, f32[512,256]{1,0:T(8,128)}, f32[512,256]{1,0:T(8,128)}) custom-call(bf16[512,512]{1,0:T(8,128)(2,1)} %tok.1, bf16[512,256]{1,0:T(8,128)(2,1)} %gw.1, bf16[512,256]{1,0:T(8,128)(2,1)} %uw.1, bf16[512,256]{1,0:T(8,128)(2,1)} %hg.1), custom_call_target="tpu_custom_call" | custom-call | tf_op jit(solution)/shard_map/pallas_call | solution.py:553
  140.6 2.7 %shard_map.76 = (bf16[512,256]{1,0:T(8,128)(2,1)}, bf16[512,512]{1,0:T(8,128)(2,1)}, f32[512,256]{1,0:T(8,128)}, f32[512,256]{1,0:T(8,128)}) custom-call(bf16[512,256]{1,0:T(8,128)(2,1)} %get-tuple-element.8.refs_0_, bf16[512,512]{1,0:T(8,128)(2,1)} %get-tuple-element.9.refs_1_, f32[512,256]{1,0:T(8,128)} %get-tuple-element.10.refs_2_, ...), custom_call_target="tpu_custom_call" | custom-call | tf_op jit(solution)/shard_map/pallas_call | solution.py:593

commit v6 on v4

--- a/solution.py
+++ b/solution.py
@@ -36,6 +36,15 @@
     barrier = pltpu.get_barrier_semaphore()
     for d in (right, left, sib, lnb, yr, yl, swap, hpeer):
         pl.semaphore_signal(barrier, inc=1, device_id=d, device_id_type=MESH)
+    for n in range(2):
+        part = slice(n * Q, (n + 1) * Q)
+        w_all[z, :, n * H:n * H + Q] = gw[:, part]
+        w_all[z, :, n * H + Q:(n + 1) * H] = uw[:, part]
+
+    @pl.when(odd == 0)
+    def _():
+        t_all[t] = tok[...]
+
     pl.semaphore_wait(barrier, 8)
 
     n_used = [0]
@@ -71,11 +80,6 @@
             body(pl.ds(start + i * 64, 64))
             return 0
         lax.fori_loop(0, size // 64, one, 0)
-
-    for n in range(2):
-        part = slice(n * Q, (n + 1) * Q)
-        w_all[z, :, n * H:n * H + Q] = gw[:, part]
-        w_all[z, :, n * H + Q:(n + 1) * H] = uw[:, part]
 
     def w_copy(way, s, half):
         out, into = ((z + 8 - s) % 8, (z + 7 - s) % 8) if way == 0 else ((z + s) % 8, (z + 1 + s) % 8)
@@ -179,7 +183,6 @@
 
     @pl.when(odd == 0)
     def _():
-        t_all[t] = tok[...]
         for k in range(4):
             own(k)
         sb[0, 0].start()

time: 143 us -> 142 us (level)
  no operation moved by 1% of the time
where the time goes in v6:
time: 142 us
  Pallas kernels  142 us (100%)
    pallas_call x1, Pallas kernels, body(): pl.pallas_call(kernel, out_shape=(jax.ShapeDtypeStruct((B, H), BF16), jax...  139 us

profile of v6, /device:TPU:26, one launch (start us, length us, event | category | flops | bytes accessed | tf_op | source)
XLA Modules:
  0.0 142.3 jit_solution(16268201583761894131)
XLA Ops:
  0.6 139.0 %shard_map.75 = (bf16[512,256]{1,0:T(8,128)(2,1)}, bf16[512,512]{1,0:T(8,128)(2,1)}, f32[512,256]{1,0:T(8,128)}, f32[512,256]{1,0:T(8,128)}) custom-call(bf16[512,512]{1,0:T(8,128)(2,1)} %tok.1, bf16[512,256]{1,0:T(8,128)(2,1)} %gw.1, bf16[512,256]{1,0:T(8,128)(2,1)} %uw.1, bf16[512,256]{1,0:T(8,128)(2,1)} %hg.1), custom_call_target="tpu_custom_call" | custom-call | tf_op jit(solution)/shard_map/pallas_call | solution.py:556
  139.6 2.7 %shard_map.76 = (bf16[512,256]{1,0:T(8,128)(2,1)}, bf16[512,512]{1,0:T(8,128)(2,1)}, f32[512,256]{1,0:T(8,128)}, f32[512,256]{1,0:T(8,128)}) custom-call(bf16[512,256]{1,0:T(8,128)(2,1)} %get-tuple-element.8.refs_0_, bf16[512,512]{1,0:T(8,128)(2,1)} %get-tuple-element.9.refs_1_, f32[512,256]{1,0:T(8,128)} %get-tuple-element.10.refs_2_, ...), custom_call_target="tpu_custom_call" | custom-call | tf_op jit(solution)/shard_map/pallas_call | solution.py:596
